TPU v7x, 256 devices: a whole 4x4x8 slice. The times are simulated.
256 devices in a mesh: ctx: 16 (over z, core), node: 4 (over y), dev: 4 (over x).
Axes of the slice: x: 4, y: 4, z: 8, core: 2. Of those that a mesh axis runs over, the one named last changes fastest.
Arguments:
- queries: bfloat16 [32, 128, 576], P('node'), may hold values from -6 to 6
- latent_cache: bfloat16 [32, 16384, 576], P('node', ('ctx', 'dev')), may hold values from -256 to 256
- block_ids: int32 [32, 32], P('node'), may hold values from 0 to 255, as said below
- value_lift_weight: bfloat16 [128, 512, 128], P(('ctx', 'dev')), may hold values from -0.25 to 0.25
- out_weight: bfloat16 [16384, 7168], P(('ctx', 'dev')), may hold values from -0.046875 to 0.046875
- residual: bfloat16 [32, 7168], P('node'), may hold values from -1.5 to 1.5
- norm_gain: bfloat16 [7168], replicated, may hold values from 0.099609375 to 1.8984375
- expert_ids: int32 [32, 8], replicated, may hold values from 0 to 15, all different within a row; in each aligned block of 8 rows (0 to 7, 8 to 15, ...) at most 6 rows name the same one
- expert_weights: float32 [32, 8], replicated, may hold values from 0.05 to 0.6
- gate_weight: bfloat16 [16, 7168, 2048], P(('node', 'dev'), None, 'ctx'), may hold values from -0.0625 to 0.0625
- up_weight: bfloat16 [16, 7168, 2048], P(('node', 'dev'), None, 'ctx'), may hold values from -0.0625 to 0.0625
- down_weight: bfloat16 [16, 2048, 7168], P(('node', 'dev'), 'ctx'), may hold values from -0.125 to 0.125
Outputs:
- layer_out: bfloat16 [32, 7168], P('node', ('ctx', 'dev'))
Inputs may be any that keep to these rules, and one draw needn't show every extreme that they name: `block_ids`: each row names 32 different blocks; at most 2 of a row's blocks lie in one part of 4 blocks, and exactly 2 in some part of every row. `expert_ids`: in each aligned block of 8 rows no expert is named by more than 6 rows.
All inputs are finite; a program needn't handle non-finite values.
Results may differ from a plain program's by a relative error of at most 0.015.
Values may be sent and summed in bfloat16 or wider, within the bound.
A program may use at most 320 MiB of HBM per device.

v0:
```python
import math

import jax
import jax.numpy as jnp
from jax import lax
from jax.experimental import pallas as pl
from jax.experimental.pallas import tpu as pltpu
from jax.sharding import PartitionSpec as P

MESH = pl.DeviceIdType.MESH
F32, BF16 = jnp.float32, jnp.bfloat16
score_scale = 192.0 ** (-0.5) * (0.1 * math.log(40.0) + 1.0) ** 2
floor_score = -1e30
norm_eps = 1e-06

PAIRS = (
    ("a1", 8), ("s1", 8), ("s2", 8), ("a2", 8), ("a3", 8), ("b1", 8),
    ("b2", 8), ("c1", 16), ("c2", 4), ("wd", 1), ("hid", 1), ("d2", 16), ("d3", 8),
)
BUFFERS = (
    ("qv", (8, 576, 128), BF16), ("cv", (8, 576, 256), BF16), ("liftv", (2, 512, 128), BF16),
    ("wov", (256, 7168), BF16), ("wguv", (7168, 256), BF16), ("wdv", (128, 7168), BF16),
    ("keep", (8, 256), F32), ("probs", (8, 128, 256), BF16),
    ("st1", (8, 16, 128), F32), ("st2", (8, 16, 128), F32), ("fcol", (128, 128), F32),
    ("a1own", (8, 64, 512), F32), ("a1snd", (8, 64, 512), BF16), ("a1rcv", (8, 64, 512), BF16),
    ("a2snd", (4, 8, 16, 512), BF16), ("a2rcv", (4, 8, 16, 512), BF16),
    ("a3snd", (8, 16, 512), BF16), ("a3rcv", (8, 16, 512), BF16),
    ("b1snd", (8, 16, 512), BF16), ("b1rcv", (8, 16, 512), BF16), ("part", (8, 16, 512), BF16),
    ("state", (32, 16, 512), BF16), ("normed", (4, 64, 512), BF16), ("gain", (8, 16, 512), F32),
    ("select", (4, 384, 256), BF16), ("laid", (2, 128, 4096), BF16), ("down", (256, 4096), BF16),
    ("hidden", (2, 32, 128), BF16), ("d2snd", (16, 4, 16, 128), BF16), ("d2rcv", (16, 4, 16, 128), BF16),
    ("d3snd", (8, 8, 128), F32), ("d3rcv", (8, 8, 128), F32),
)


class Names:
    pass


def dot(a, b, dims=((1,), (0,))):
    return lax.dot_general(a, b, (dims, ((), ())), preferred_element_type=F32)


def iota(shape, dim):
    return lax.broadcasted_iota(jnp.int32, shape, dim)


def kernel(ids_ref, gain_ref, eid_ref, ew_ref, res_ref, q_hbm, c_hbm, lift_hbm, wo_hbm, wg_hbm, wu_hbm, wd_hbm,
           out_ref, *scratch):
    v = Names()
    for (name, _, _), ref in zip(BUFFERS, scratch):
        setattr(v, name, ref)
    rest = scratch[len(BUFFERS):]
    local = rest[0]
    sems = {name: (rest[1 + 2 * i], rest[2 + 2 * i]) for i, (name, _) in enumerate(PAIRS)}

    ctx, node, dev = lax.axis_index("ctx"), lax.axis_index("node"), lax.axis_index("dev")
    z, core = lax.div(ctx, 2), lax.rem(ctx, 2)
    other = 1 - core
    g = core * 4 + dev
    shard = ctx * 4 + dev
    expert = node * 4 + dev

    def turn(a, k, n):
        return lax.rem(a + k, n)

    def at(ctx=ctx, node=node, dev=dev):
        return {"ctx": ctx, "node": node, "dev": dev}

    def at_core():
        return at(ctx=z * 2 + other)

    def at_z(k):
        return at(ctx=turn(z, k, 8) * 2 + core)

    def at_g(k):
        there = turn(g, k, 8)
        return at(ctx=z * 2 + lax.div(there, 4), dev=lax.rem(there, 4))

    def remote(name, slot, src, dst, where):
        send, recv = sems[name]
        return pltpu.make_async_remote_copy(
            src_ref=src, dst_ref=dst, send_sem=send.at[slot], recv_sem=recv.at[slot],
            device_id=where, device_id_type=MESH,
        )

    sent, fetches = [], []

    def push(*args):
        copy = remote(*args)
        copy.start()
        sent.append(copy)
        return copy

    far_z, far_g = (4, 3, 5, 2, 6, 1, 7), (2, 6, 1, 3, 5, 7, 4)

    def hops(i, j):
        return min(i, 4 - i) + min(j, 4 - j)

    far_xy = sorted(((i, j) for i in range(4) for j in range(4) if i + j), key=lambda step: -hops(*step))

    def fetch_q(r):
        return pltpu.make_async_copy(q_hbm.at[r], v.qv.at[r], local.at[r])

    def fetch_c(r):
        return pltpu.make_async_copy(c_hbm.at[r], v.cv.at[r], local.at[8 + r])

    for i in range(8):
        fetch_q(i).start()
        fetch_c(i).start()
    fetch_lift = pltpu.make_async_copy(lift_hbm, v.liftv, local.at[16])
    fetch_wo = pltpu.make_async_copy(wo_hbm, v.wov, local.at[17])
    fetch_wg = pltpu.make_async_copy(wg_hbm.at[0], v.wguv.at[:, pl.ds(0, 128)], local.at[18])
    fetch_wu = pltpu.make_async_copy(wu_hbm.at[0], v.wguv.at[:, pl.ds(128, 128)], local.at[19])
    fetch_wd = pltpu.make_async_copy(wd_hbm.at[0], v.wdv, local.at[20])
    for copy in (fetch_lift, fetch_wo, fetch_wg, fetch_wu, fetch_wd):
        copy.start()
        fetches.append(copy)

    def ready(*copies):
        for copy in copies:
            fetches[:] = [other_copy for other_copy in fetches if other_copy is not copy]
            copy.wait()

    barrier = pltpu.get_barrier_semaphore()
    partners = [(min(k, 8 - k), at_z(k)) for k in far_z]
    partners += [(2 if k in (2, 6) else k % 2, at_g(k)) for k in far_g]
    partners += [(hops(i, j), at(node=turn(node, i, 4), dev=turn(dev, j, 4))) for i in range(1, 4) for j in range(4)]
    for _, where in sorted(partners, key=lambda partner: -partner[0]):
        pl.semaphore_signal(barrier, inc=1, device_id=where, device_id_type=MESH)

    ids = ids_ref[...]
    block = lax.div(iota((8, 256), 1), 64)
    keep = jnp.zeros((8, 256), F32)
    for b in range(4):
        hit = jnp.max(jnp.where(ids == shard * 4 + b, 1.0, 0.0), axis=1, keepdims=True)
        keep = jnp.where(block == b, hit, keep)
    v.keep[...] = keep

    def one_hot(hit):
        return jnp.where(hit, 1.0, 0.0).astype(BF16)

    at_row, at_col = iota((128, 128), 0), iota((128, 128), 1)

    def part_of(number, low, size):
        return lax.rem(lax.div(number, low), size)

    by_owner = one_hot(
        at_col == part_of(at_row, 2, 8) * 16 + part_of(at_row, 64, 2) * 8 + part_of(at_row, 16, 4) * 2 + part_of(at_row, 1, 2)
    )
    stats = jnp.zeros((128, 128), F32)
    for r in range(8):
        fetch_q(r).wait()
        fetch_c(r).wait()
        kept = v.keep[r:r + 1, :] > 0.5
        heads = dot(by_owner, v.qv[r], ((1,), (1,))).astype(BF16)
        scores = dot(heads, v.cv[r]) * score_scale
        scores = jnp.where(kept, scores, floor_score)
        top = jnp.max(scores, axis=1, keepdims=True)
        probs = jnp.where(kept, jnp.exp(scores - top), 0.0).astype(BF16)
        total = jnp.sum(probs.astype(F32), axis=1, keepdims=True)
        v.probs[r] = probs
        stats = jnp.where(at_col == r, top, jnp.where(at_col == r + 8, total, stats))
    stats = stats.T[:16, :]

    for r in range(8):
        num = dot(v.probs[r], v.cv[r, :512, :], ((1,), (1,)))
        v.a1snd[r] = jnp.where(core == 0, num[64:], num[:64]).astype(BF16)
        v.a1own[r] = jnp.where(core == 0, num[:64], num[64:])
    v.st1[g] = stats
    pl.semaphore_wait(barrier, len(partners))
    s1 = {k: push("s1", k, v.st1.at[g], v.st1.at[g], at_g(k)) for k in (4,) + far_g[:6]}
    a1 = [push("a1", r, v.a1snd.at[r], v.a1rcv.at[r], at_core()) for r in range(8)]

    def joined(ref):
        peak = ref[0, :8, :]
        for i in range(1, 8):
            peak = jnp.maximum(peak, ref[i, :8, :])
        total = jnp.zeros((8, 128), F32)
        for i in range(8):
            total += ref[i, 8:, :] * jnp.exp(ref[i, :8, :] - peak)
        return peak, total

    def pair_top(x):
        return jnp.maximum(v.st1[x, :8, :], v.st1[4 + x, :8, :])

    s1.pop(4).wait_recv()
    pair = pair_top(dev)
    here = jnp.exp(v.st1[g, :8, :] - pair)
    there = jnp.exp(v.st1[other * 4 + dev, :8, :] - pair)
    v.fcol[...] = jnp.concatenate([here, there, jnp.zeros((112, 128), F32)], axis=0).T

    half = pl.ds(pl.multiple_of(core * 64, 64), 64)
    a2 = []
    for r in range(8):
        a1[r].wait_recv()
        both = v.fcol[half, r:r + 1] * v.a1own[r] + v.fcol[half, r + 8:r + 9] * v.a1rcv[r].astype(F32)
        both = both.astype(BF16)
        for x in range(4):
            v.a2snd[x, r] = both[x * 16:x * 16 + 16]
        if r % 4 == 3:
            chunk = pl.ds(r - 3, 4)
            for k in (2, 1, 3):
                xt = turn(dev, k, 4)
                a2.append(push("a2", k + r // 4 * 4, v.a2snd.at[xt, chunk], v.a2rcv.at[k, chunk], at(dev=xt)))
    for copy in s1.values():
        copy.wait_recv()
    peak, total = joined(v.st1)
    v.st2[z, :8, :] = peak
    v.st2[z, 8:, :] = total
    s2 = [push("s2", k, v.st2.at[z], v.st2.at[z], at_z(k)) for k in far_z]

    spans = ((0, 256), (128, 384), (384, 384), (640, 256))
    into, outof = iota((384, 256), 1), iota((384, 256), 0)
    for i, (first, _) in enumerate(spans):
        source = i * 224 - first + lax.div(into, 128) * 112 + lax.rem(into, 128)
        v.select[i] = one_hot((outof == source) & (lax.rem(into, 128) < 112))

    def lay_out(blocks):
        for zt in blocks:
            for i, (first, width) in enumerate(spans):
                columns = v.wdv[:, zt * 896 + first:zt * 896 + first + width]
                piece = dot(columns, v.select[i, :width, :]).astype(BF16)
                v.laid[i // 2, :, zt * 512 + i % 2 * 256:zt * 512 + i % 2 * 256 + 256] = piece

    ready(fetch_wd)
    lay_out(range(4))
    for copy in s2:
        copy.wait_recv()
    peak, total = joined(v.st2)
    factors = [jnp.exp(pair_top(turn(dev, 4 - k, 4)) - peak) / total for k in range(4)]
    v.fcol[...] = jnp.concatenate(factors + [jnp.zeros((96, 128), F32)], axis=0).T

    sixteen = pl.ds(pl.multiple_of(core * 64 + dev * 16, 16), 16)
    by_z = one_hot(at_col == part_of(at_row, 1, 8) * 16 + part_of(at_row, 16, 8) * 2 + part_of(at_row, 8, 2))
    latents = jnp.zeros((128, 512), F32)
    for c in range(2):
        for copy in a2[3 * c:3 * c + 3]:
            copy.wait_recv()
        rows = []
        for r in range(4 * c, 4 * c + 4):
            row = v.fcol[sixteen, r:r + 1] * v.a2snd[dev, r].astype(F32)
            for k in range(1, 4):
                row += v.fcol[sixteen, k * 8 + r:k * 8 + r + 1] * v.a2rcv[k, r].astype(F32)
            rows.append(row.astype(BF16))
        latents += dot(by_z[:, c * 64:c * 64 + 64], jnp.concatenate(rows, axis=0))

    v.a3snd[...] = latents.astype(BF16).reshape(8, 16, 512)
    a3 = []
    for k in far_z:
        zt = turn(z, k, 8)
        a3.append((k, push("a3", k, v.a3snd.at[zt], v.a3rcv.at[k], at_z(k))))
    for i in range(8):
        for t in range(4):
            row = i * 7 + t
            v.gain[i, :8, t * 128:t * 128 + 128] = jnp.broadcast_to(gain_ref[row:row + 1, :].astype(F32), (8, 128))
            v.gain[i, 8:, t * 128:t * 128 + 128] = jnp.broadcast_to(gain_ref[row + 3:row + 4, :].astype(F32), (8, 128))
    lay_out(range(4, 8))
    mine_rows = pl.ds(pl.multiple_of(core * 128, 128), 128)
    wd = push("wd", 0, v.laid.at[other], v.down.at[mine_rows], at_core())
    keep_wd = pltpu.make_async_copy(v.laid.at[core], v.down.at[mine_rows], local.at[21])
    keep_wd.start()
    fetches.append(keep_wd)
    ready(fetch_lift, fetch_wo)
    summed = v.a3snd[z].astype(F32)
    for k, copy in a3:
        copy.wait_recv()
        summed += v.a3rcv[k].astype(F32)
    own_heads = summed.astype(BF16)
    values = jnp.concatenate([dot(own_heads, v.liftv[0])[:8], dot(own_heads, v.liftv[1])[8:]], axis=1).astype(BF16)

    def projected(i):
        upper = dot(values, v.wov[:, pl.ds(pl.multiple_of(i * 896, 128), 512)])
        lower = dot(values, v.wov[:, pl.ds(pl.multiple_of(i * 896 + 512, 128), 384)])
        return jnp.concatenate([upper, jnp.concatenate([upper[:, 384:], lower], axis=1)], axis=0)

    b1 = []
    for k in far_g:
        gt = turn(g, k, 8)
        v.b1snd[gt] = projected(gt).astype(BF16)
        b1.append((k, push("b1", k, v.b1snd.at[gt], v.b1rcv.at[k], at_g(k))))
    summed = projected(g)
    residual = jnp.concatenate(
        [
            res_ref[:, pl.ds(pl.multiple_of(g * 896, 128), 512)].astype(F32),
            res_ref[:, pl.ds(pl.multiple_of(g * 896 + 384, 128), 512)].astype(F32),
        ],
        axis=0,
    )
    for k, copy in b1:
        copy.wait_recv()
        summed += v.b1rcv[k].astype(F32)
    v.part[z] = summed.astype(BF16)
    b2 = [push("b2", k, v.part.at[z], v.part.at[z], at_z(k)) for k in far_z]
    ready(fetch_wg, fetch_wu)
    for copy in b2:
        copy.wait_recv()
    attention = v.part[0].astype(F32)
    for i in range(1, 8):
        attention += v.part[i].astype(F32)
    mine = core * 16 + node * 4 + dev
    v.state[mine] = (residual + attention).astype(BF16)

    c1, c2 = {}, []
    for i, j in far_xy:
        where = at(node=turn(node, i, 4), dev=turn(dev, j, 4))
        c1[i, j] = push("c1", i * 4 + j, v.state.at[mine], v.state.at[mine], where)
    coef = jnp.sum(jnp.where(eid_ref[...] == expert, ew_ref[...], 0.0), axis=0, keepdims=True)
    coef = jnp.sum(jnp.where(iota((32, 32), 0) == iota((32, 32), 1), coef, 0.0), axis=1, keepdims=True)
    for i in (0, 1, 3, 2):
        for j in range(4):
            if i + j > 0:
                c1[i, j].wait_recv()
        came = pl.ds(core * 16 + turn(node, 4 - i, 4) * 4, 4)
        c2.append(push("c2", i, v.state.at[came], v.state.at[came], at_core()))

    squares = [jnp.zeros((16, 512), F32) for _ in range(4)]
    upper = jnp.zeros((64, 256), F32)
    lower = jnp.zeros((64, 256), F32)
    for c in (core, other):
        for i in range(4):
            block = c * 4 + i
            for y in range(4):
                wide = v.state[c * 16 + y * 4 + i].astype(F32)
                squares[y] += wide * wide
                v.normed[i, y * 16:y * 16 + 16, :] = (wide * v.gain[block]).astype(BF16)
            first = pl.multiple_of(block * 896, 128)
            upper += dot(v.normed[i], v.wguv[pl.ds(first, 512), :])
            lower += dot(v.normed[i, :, 128:], v.wguv[pl.ds(first + 512, 384), :])
        if c is core:
            for copy in c2:
                copy.wait_recv()
    once = (iota((16, 512), 0) < 8) | (iota((16, 512), 1) >= 128)
    scale = []
    for y in range(4):
        square = jnp.sum(jnp.where(once, squares[y], 0.0), axis=1, keepdims=True)
        scale.append(lax.rsqrt((square[:8] + square[8:]) / 7168.0 + norm_eps))
    both = jnp.concatenate([upper[y * 16:y * 16 + 8] + lower[y * 16 + 8:y * 16 + 16] for y in range(4)], axis=0)
    both = both * jnp.concatenate(scale, axis=0)
    gate, up = both[:, :128], both[:, 128:]
    v.hidden[core] = (gate / (1.0 + jnp.exp(-gate)) * up * coef).astype(BF16)
    hid = push("hid", 0, v.hidden.at[core], v.hidden.at[core], at_core())

    own = v.state[lax.div(z, 4) * 16 + node * 4 + lax.rem(z, 4)]
    own = dot(own, one_hot(iota((512, 128), 0) == iota((512, 128), 1) + core * 64 + dev * 112))
    own = jnp.where(core == 0, own[:8], own[8:])

    ready(keep_wd)
    wd.wait_recv()
    hid.wait_recv()
    hidden = jnp.concatenate([v.hidden[0], v.hidden[1]], axis=1)
    for i in range(4):
        first = dot(hidden, v.down[:, i * 1024:i * 1024 + 512])
        second = dot(hidden, v.down[:, i * 1024 + 512:i * 1024 + 1024])
        for y in range(4):
            pair = jnp.concatenate([first[y * 8:y * 8 + 8], second[y * 8:y * 8 + 8]], axis=0).astype(BF16)
            for x in range(4):
                v.d2snd[y * 4 + x, i] = pair[:, x * 128:x * 128 + 128]
    d2 = []
    for i, j in far_xy:
        yt, xt = turn(node, i, 4), turn(dev, j, 4)
        d2.append((i * 4 + j, push("d2", i * 4 + j, v.d2snd.at[yt * 4 + xt], v.d2rcv.at[i * 4 + j], at(node=yt, dev=xt))))
    mixture = [v.d2snd[node * 4 + dev, i].astype(F32) for i in range(4)]
    for k, copy in reversed(d2):
        copy.wait_recv()
        for i in range(4):
            mixture[i] += v.d2rcv[k, i].astype(F32)
    for i in range(4):
        v.d3snd[2 * i] = mixture[i][:8]
        v.d3snd[2 * i + 1] = mixture[i][8:]
    d3 = []
    for k in far_z:
        d3.append((k, push("d3", k, v.d3snd.at[turn(z, k, 8)], v.d3rcv.at[k], at_z(k))))
    mixture = v.d3snd[z]
    for k, copy in reversed(d3):
        copy.wait_recv()
        mixture += v.d3rcv[k]
    out_ref[...] = (own + mixture).astype(BF16)[:, :112]

    for copy in sent:
        copy.wait_send()


def shards(queries, latent_cache, block_ids, value_lift_weight, out_weight, residual, norm_gain, expert_ids,
           expert_weights, gate_weight, up_weight, down_weight):
    vmem, anywhere = pl.BlockSpec(memory_space=pltpu.VMEM), pl.BlockSpec(memory_space=pl.ANY)
    scratch = [pltpu.VMEM(shape, dtype) for _, shape, dtype in BUFFERS]
    scratch.append(pltpu.SemaphoreType.DMA((22,)))
    for _, count in PAIRS:
        scratch += [pltpu.SemaphoreType.DMA((count,)), pltpu.SemaphoreType.DMA((count,))]
    return pl.pallas_call(
        kernel,
        out_shape=jax.ShapeDtypeStruct((8, 112), BF16),
        in_specs=[vmem] * 5 + [anywhere] * 7,
        out_specs=vmem,
        scratch_shapes=scratch,
        compiler_params=pltpu.CompilerParams(
            collective_id=0, has_side_effects=True, vmem_limit_bytes=56 * 1024 * 1024
        ),
        name="layer",
    )(
        block_ids, norm_gain.reshape(56, 128), expert_ids.T, expert_weights.T, residual,
        jnp.swapaxes(queries, 1, 2), jnp.swapaxes(latent_cache, 1, 2),
        value_lift_weight, out_weight, gate_weight, up_weight, down_weight,
    )


def solution(mesh):
    placed = (
        P("node", None, None),
        P("node", ("ctx", "dev"), None),
        P("node", None),
        P(("ctx", "dev"), None, None),
        P(("ctx", "dev"), None),
        P("node", None),
        P(),
        P(),
        P(),
        P(("node", "dev"), None, "ctx"),
        P(("node", "dev"), None, "ctx"),
        P(("node", "dev"), "ctx", None),
    )
    return jax.shard_map(
        shards, mesh=mesh, in_specs=placed, out_specs=P("node", ("ctx", "dev")), check_vma=False
    )
```

profile of v0, /device:TPU:2, one launch (start us, length us, event | category | flops | bytes accessed | tf_op | source)
XLA Modules:
  0.0 59.6 jit_solution(18365662787679938887)
XLA Ops:
  0.0 58.3 %layer.1 = bf16[8,112]{1,0:T(8,128)(2,1)} custom-call(s32[8,32]{1,0:T(8,128)} %ids_ref.1, bf16[56,128]{1,0:T(8,128)(2,1)} %bitcast.7, s32[8,32]{1,0:T(8,128)} %bitcast.8, f32[8,32]{1,0:T(8,128)} %bitcast.9, bf16[8,7168]{1,0:T(8,128)(2,1)} %res_ref.1, bf16[8,576,128]{2,1,0:T(8,128)(2,1)} %bitcast.6, bf16[8,576,256]{2,1,0:T(8,128)(2,1)} %bitcast.5, ...), custom_call_target="tpu_custom_call" | custom-call | tf_op jit(solution)/shard_map/layer/pallas_call | solution.py:391
  58.3 1.3 %copy.14 = bf16[8,112]{1,0:T(8,128)(2,1)} copy(bf16[8,112]{1,0:T(8,128)(2,1)} %layer.1) | data formatting | bytes 3584
where the time goes:
time: 59.8 us; the launch traced here: 59.6 us
  Pallas kernels  58.3 us (97%)
  local copies, waits for them, and re-layouts  1.26 us (2%)
    pallas_call x1, Pallas kernels, shards(): pl.pallas_call(kernel, out_shape=jax.ShapeDtypeStruct((8, 112), BF16), in...  58.3 us
    unnamed x1, local copies, waits for them, and re-layouts  1.26 us

commit v1 on v0

--- a/solution.py
+++ b/solution.py
@@ -18,7 +18,8 @@
     ("b2", 8), ("c1", 16), ("c2", 4), ("wd", 1), ("hid", 1), ("d2", 16), ("d3", 8),
 )
 BUFFERS = (
-    ("qv", (8, 576, 128), BF16), ("cv", (8, 576, 256), BF16), ("liftv", (2, 512, 128), BF16),
+    ("ids", (8, 32), jnp.int32), ("gain_in", (56, 128), BF16), ("eid", (8, 32), jnp.int32), ("ew", (8, 32), F32),
+    ("res", (8, 7168), BF16), ("qv", (8, 576, 128), BF16), ("cv", (8, 576, 256), BF16), ("liftv", (2, 512, 128), BF16),
     ("wov", (256, 7168), BF16), ("wguv", (7168, 256), BF16), ("wdv", (128, 7168), BF16),
     ("keep", (8, 256), F32), ("probs", (8, 128, 256), BF16),
     ("st1", (8, 16, 128), F32), ("st2", (8, 16, 128), F32), ("fcol", (128, 128), F32),
@@ -33,6 +34,11 @@
 )
 
 
+ROWS_AT_ONCE = 4
+SENT_AT_ONCE = 4
+BLOCKS_AT_ONCE = 4
+
+
 class Names:
     pass
 
@@ -45,7 +51,7 @@
     return lax.broadcasted_iota(jnp.int32, shape, dim)
 
 
-def kernel(ids_ref, gain_ref, eid_ref, ew_ref, res_ref, q_hbm, c_hbm, lift_hbm, wo_hbm, wg_hbm, wu_hbm, wd_hbm,
+def kernel(ids_hbm, gain_hbm, eid_hbm, ew_hbm, res_hbm, q_hbm, c_hbm, lift_hbm, wo_hbm, wg_hbm, wu_hbm, wd_hbm,
            out_ref, *scratch):
     v = Names()
     for (name, _, _), ref in zip(BUFFERS, scratch):
@@ -99,29 +105,6 @@
 
     far_xy = sorted(((i, j) for i in range(4) for j in range(4) if i + j), key=lambda step: -hops(*step))
 
-    def fetch_q(r):
-        return pltpu.make_async_copy(q_hbm.at[r], v.qv.at[r], local.at[r])
-
-    def fetch_c(r):
-        return pltpu.make_async_copy(c_hbm.at[r], v.cv.at[r], local.at[8 + r])
-
-    for i in range(8):
-        fetch_q(i).start()
-        fetch_c(i).start()
-    fetch_lift = pltpu.make_async_copy(lift_hbm, v.liftv, local.at[16])
-    fetch_wo = pltpu.make_async_copy(wo_hbm, v.wov, local.at[17])
-    fetch_wg = pltpu.make_async_copy(wg_hbm.at[0], v.wguv.at[:, pl.ds(0, 128)], local.at[18])
-    fetch_wu = pltpu.make_async_copy(wu_hbm.at[0], v.wguv.at[:, pl.ds(128, 128)], local.at[19])
-    fetch_wd = pltpu.make_async_copy(wd_hbm.at[0], v.wdv, local.at[20])
-    for copy in (fetch_lift, fetch_wo, fetch_wg, fetch_wu, fetch_wd):
-        copy.start()
-        fetches.append(copy)
-
-    def ready(*copies):
-        for copy in copies:
-            fetches[:] = [other_copy for other_copy in fetches if other_copy is not copy]
-            copy.wait()
-
     barrier = pltpu.get_barrier_semaphore()
     partners = [(min(k, 8 - k), at_z(k)) for k in far_z]
     partners += [(2 if k in (2, 6) else k % 2, at_g(k)) for k in far_g]
@@ -129,7 +112,37 @@
     for _, where in sorted(partners, key=lambda partner: -partner[0]):
         pl.semaphore_signal(barrier, inc=1, device_id=where, device_id_type=MESH)
 
-    ids = ids_ref[...]
+    def fetch_q(r):
+        return pltpu.make_async_copy(q_hbm.at[r], v.qv.at[r], local.at[r])
+
+    def fetch_c(r):
+        return pltpu.make_async_copy(c_hbm.at[r], v.cv.at[r], local.at[8 + r])
+
+    fetch_ids = pltpu.make_async_copy(ids_hbm, v.ids, local.at[22])
+    fetch_ids.start()
+    for i in range(8):
+        fetch_q(i).start()
+        fetch_c(i).start()
+    fetch_gain = pltpu.make_async_copy(gain_hbm, v.gain_in, local.at[23])
+    fetch_eid = pltpu.make_async_copy(eid_hbm, v.eid, local.at[24])
+    fetch_ew = pltpu.make_async_copy(ew_hbm, v.ew, local.at[25])
+    fetch_res = pltpu.make_async_copy(res_hbm, v.res, local.at[26])
+    fetch_lift = pltpu.make_async_copy(lift_hbm, v.liftv, local.at[16])
+    fetch_wo = pltpu.make_async_copy(wo_hbm, v.wov, local.at[17])
+    fetch_wg = pltpu.make_async_copy(wg_hbm.at[0], v.wguv.at[:, pl.ds(0, 128)], local.at[18])
+    fetch_wu = pltpu.make_async_copy(wu_hbm.at[0], v.wguv.at[:, pl.ds(128, 128)], local.at[19])
+    fetch_wd = pltpu.make_async_copy(wd_hbm.at[0], v.wdv, local.at[20])
+    for copy in (fetch_gain, fetch_eid, fetch_ew, fetch_res, fetch_wd, fetch_lift, fetch_wo, fetch_wg, fetch_wu):
+        copy.start()
+        fetches.append(copy)
+
+    def ready(*copies):
+        for copy in copies:
+            fetches[:] = [other_copy for other_copy in fetches if other_copy is not copy]
+            copy.wait()
+
+    fetch_ids.wait()
+    ids = v.ids[...]
     block = lax.div(iota((8, 256), 1), 64)
     keep = jnp.zeros((8, 256), F32)
     for b in range(4):
@@ -150,8 +163,10 @@
     )
     stats = jnp.zeros((128, 128), F32)
     for r in range(8):
-        fetch_q(r).wait()
-        fetch_c(r).wait()
+        if r % ROWS_AT_ONCE == 0:
+            for i in range(r, r + ROWS_AT_ONCE):
+                fetch_q(i).wait()
+                fetch_c(i).wait()
         kept = v.keep[r:r + 1, :] > 0.5
         heads = dot(by_owner, v.qv[r], ((1,), (1,))).astype(BF16)
         scores = dot(heads, v.cv[r]) * score_scale
@@ -163,14 +178,18 @@
         stats = jnp.where(at_col == r, top, jnp.where(at_col == r + 8, total, stats))
     stats = stats.T[:16, :]
 
+    v.st1[g] = stats
+    pl.semaphore_wait(barrier, len(partners))
+    s1 = {k: push("s1", k, v.st1.at[g], v.st1.at[g], at_g(k)) for k in (4,) + far_g[:6]}
+
+    a1 = []
     for r in range(8):
         num = dot(v.probs[r], v.cv[r, :512, :], ((1,), (1,)))
         v.a1snd[r] = jnp.where(core == 0, num[64:], num[:64]).astype(BF16)
         v.a1own[r] = jnp.where(core == 0, num[:64], num[64:])
-    v.st1[g] = stats
-    pl.semaphore_wait(barrier, len(partners))
-    s1 = {k: push("s1", k, v.st1.at[g], v.st1.at[g], at_g(k)) for k in (4,) + far_g[:6]}
-    a1 = [push("a1", r, v.a1snd.at[r], v.a1rcv.at[r], at_core()) for r in range(8)]
+        if r % SENT_AT_ONCE == SENT_AT_ONCE - 1:
+            for i in range(r + 1 - SENT_AT_ONCE, r + 1):
+                a1.append(push("a1", i, v.a1snd.at[i], v.a1rcv.at[i], at_core()))
 
     def joined(ref):
         peak = ref[0, :8, :]
@@ -193,7 +212,9 @@
     half = pl.ds(pl.multiple_of(core * 64, 64), 64)
     a2 = []
     for r in range(8):
-        a1[r].wait_recv()
+        if r % 4 == 0:
+            for copy in a1[r:r + 4]:
+                copy.wait_recv()
         both = v.fcol[half, r:r + 1] * v.a1own[r] + v.fcol[half, r + 8:r + 9] * v.a1rcv[r].astype(F32)
         both = both.astype(BF16)
         for x in range(4):
@@ -203,12 +224,12 @@
             for k in (2, 1, 3):
                 xt = turn(dev, k, 4)
                 a2.append(push("a2", k + r // 4 * 4, v.a2snd.at[xt, chunk], v.a2rcv.at[k, chunk], at(dev=xt)))
-    for copy in s1.values():
-        copy.wait_recv()
-    peak, total = joined(v.st1)
-    v.st2[z, :8, :] = peak
-    v.st2[z, 8:, :] = total
-    s2 = [push("s2", k, v.st2.at[z], v.st2.at[z], at_z(k)) for k in far_z]
+    ready(fetch_gain)
+    for i in range(8):
+        for t in range(4):
+            row = i * 7 + t
+            v.gain[i, :8, t * 128:t * 128 + 128] = jnp.broadcast_to(v.gain_in[row:row + 1, :].astype(F32), (8, 128))
+            v.gain[i, 8:, t * 128:t * 128 + 128] = jnp.broadcast_to(v.gain_in[row + 3:row + 4, :].astype(F32), (8, 128))
 
     spans = ((0, 256), (128, 384), (384, 384), (640, 256))
     into, outof = iota((384, 256), 1), iota((384, 256), 0)
@@ -223,13 +244,17 @@
                 piece = dot(columns, v.select[i, :width, :]).astype(BF16)
                 v.laid[i // 2, :, zt * 512 + i % 2 * 256:zt * 512 + i % 2 * 256 + 256] = piece
 
+    for copy in s1.values():
+        copy.wait_recv()
+    peak, total = joined(v.st1)
+    v.st2[z, :8, :] = peak
+    v.st2[z, 8:, :] = total
+    s2 = [push("s2", k, v.st2.at[z], v.st2.at[z], at_z(k)) for k in far_z]
+
+    factors = [jnp.exp(pair_top(turn(dev, 4 - k, 4)) - peak) for k in range(4)]
+    v.fcol[...] = jnp.concatenate(factors + [jnp.zeros((96, 128), F32)], axis=0).T
     ready(fetch_wd)
-    lay_out(range(4))
-    for copy in s2:
-        copy.wait_recv()
-    peak, total = joined(v.st2)
-    factors = [jnp.exp(pair_top(turn(dev, 4 - k, 4)) - peak) / total for k in range(4)]
-    v.fcol[...] = jnp.concatenate(factors + [jnp.zeros((96, 128), F32)], axis=0).T
+    lay_out(range(2))
 
     sixteen = pl.ds(pl.multiple_of(core * 64 + dev * 16, 16), 16)
     by_z = one_hot(at_col == part_of(at_row, 1, 8) * 16 + part_of(at_row, 16, 8) * 2 + part_of(at_row, 8, 2))
@@ -250,48 +275,61 @@
     for k in far_z:
         zt = turn(z, k, 8)
         a3.append((k, push("a3", k, v.a3snd.at[zt], v.a3rcv.at[k], at_z(k))))
-    for i in range(8):
-        for t in range(4):
-            row = i * 7 + t
-            v.gain[i, :8, t * 128:t * 128 + 128] = jnp.broadcast_to(gain_ref[row:row + 1, :].astype(F32), (8, 128))
-            v.gain[i, 8:, t * 128:t * 128 + 128] = jnp.broadcast_to(gain_ref[row + 3:row + 4, :].astype(F32), (8, 128))
-    lay_out(range(4, 8))
+    lay_out(range(2, 5))
+    ready(fetch_lift, fetch_wo)
+    for copy in s2:
+        copy.wait_recv()
+    peak, total = joined(v.st2)
+
+    own_lane = iota((8, 128), 1) - (core * 64 + dev * 16 + z * 2)
+
+    def factor_of(zt):
+        factor = jnp.exp(v.st2[zt, :8, :] - peak) / total
+        columns = [jnp.sum(jnp.where(own_lane == h, factor, 0.0), axis=1, keepdims=True) for h in range(2)]
+        return jnp.concatenate(columns, axis=0)
+
+    factors = [factor_of(turn(z, 8 - k, 8)) for k in range(8)]
+    summed = factors[0] * v.a3snd[z].astype(F32)
+    for _, copy in reversed(a3):
+        copy.wait_recv()
+    for k in range(1, 8):
+        summed += factors[k] * v.a3rcv[k].astype(F32)
+    own_heads = summed.astype(BF16)
+    values = jnp.concatenate([dot(own_heads, v.liftv[0])[:8], dot(own_heads, v.liftv[1])[8:]], axis=1).astype(BF16)
+
+    def projected(i):
+        upper = dot(values, v.wov[:, pl.ds(pl.multiple_of(i * 896, 128), 512)])
+        lower = dot(values, v.wov[:, pl.ds(pl.multiple_of(i * 896 + 512, 128), 384)])
+        return jnp.concatenate([upper, jnp.concatenate([upper[:, 384:], lower], axis=1)], axis=0)
+
+    b1 = []
+    for i in range(0, 7, BLOCKS_AT_ONCE):
+        for k in far_g[i:i + BLOCKS_AT_ONCE]:
+            gt = turn(g, k, 8)
+            v.b1snd[gt] = projected(gt).astype(BF16)
+        for k in far_g[i:i + BLOCKS_AT_ONCE]:
+            b1.append((k, push("b1", k, v.b1snd.at[turn(g, k, 8)], v.b1rcv.at[k], at_g(k))))
+    summed = projected(g)
+    ready(fetch_res)
+    residual = jnp.concatenate(
+        [
+            v.res[:, pl.ds(pl.multiple_of(g * 896, 128), 512)].astype(F32),
+            v.res[:, pl.ds(pl.multiple_of(g * 896 + 384, 128), 512)].astype(F32),
+        ],
+        axis=0,
+    )
+    for _, copy in reversed(b1):
+        copy.wait_recv()
+    for k in range(1, 8):
+        summed += v.b1rcv[k].astype(F32)
+    v.part[z] = summed.astype(BF16)
+    b2 = [push("b2", k, v.part.at[z], v.part.at[z], at_z(k)) for k in far_z]
+    lay_out(range(5, 8))
     mine_rows = pl.ds(pl.multiple_of(core * 128, 128), 128)
     wd = push("wd", 0, v.laid.at[other], v.down.at[mine_rows], at_core())
     keep_wd = pltpu.make_async_copy(v.laid.at[core], v.down.at[mine_rows], local.at[21])
     keep_wd.start()
     fetches.append(keep_wd)
-    ready(fetch_lift, fetch_wo)
-    summed = v.a3snd[z].astype(F32)
-    for k, copy in a3:
-        copy.wait_recv()
-        summed += v.a3rcv[k].astype(F32)
-    own_heads = summed.astype(BF16)
-    values = jnp.concatenate([dot(own_heads, v.liftv[0])[:8], dot(own_heads, v.liftv[1])[8:]], axis=1).astype(BF16)
-
-    def projected(i):
-        upper = dot(values, v.wov[:, pl.ds(pl.multiple_of(i * 896, 128), 512)])
-        lower = dot(values, v.wov[:, pl.ds(pl.multiple_of(i * 896 + 512, 128), 384)])
-        return jnp.concatenate([upper, jnp.concatenate([upper[:, 384:], lower], axis=1)], axis=0)
-
-    b1 = []
-    for k in far_g:
-        gt = turn(g, k, 8)
-        v.b1snd[gt] = projected(gt).astype(BF16)
-        b1.append((k, push("b1", k, v.b1snd.at[gt], v.b1rcv.at[k], at_g(k))))
-    summed = projected(g)
-    residual = jnp.concatenate(
-        [
-            res_ref[:, pl.ds(pl.multiple_of(g * 896, 128), 512)].astype(F32),
-            res_ref[:, pl.ds(pl.multiple_of(g * 896 + 384, 128), 512)].astype(F32),
-        ],
-        axis=0,
-    )
-    for k, copy in b1:
-        copy.wait_recv()
-        summed += v.b1rcv[k].astype(F32)
-    v.part[z] = summed.astype(BF16)
-    b2 = [push("b2", k, v.part.at[z], v.part.at[z], at_z(k)) for k in far_z]
     ready(fetch_wg, fetch_wu)
     for copy in b2:
         copy.wait_recv()
@@ -305,7 +343,8 @@
     for i, j in far_xy:
         where = at(node=turn(node, i, 4), dev=turn(dev, j, 4))
         c1[i, j] = push("c1", i * 4 + j, v.state.at[mine], v.state.at[mine], where)
-    coef = jnp.sum(jnp.where(eid_ref[...] == expert, ew_ref[...], 0.0), axis=0, keepdims=True)
+    ready(fetch_eid, fetch_ew)
+    coef = jnp.sum(jnp.where(v.eid[...] == expert, v.ew[...], 0.0), axis=0, keepdims=True)
     coef = jnp.sum(jnp.where(iota((32, 32), 0) == iota((32, 32), 1), coef, 0.0), axis=1, keepdims=True)
     for i in (0, 1, 3, 2):
         for j in range(4):
@@ -361,8 +400,9 @@
         yt, xt = turn(node, i, 4), turn(dev, j, 4)
         d2.append((i * 4 + j, push("d2", i * 4 + j, v.d2snd.at[yt * 4 + xt], v.d2rcv.at[i * 4 + j], at(node=yt, dev=xt))))
     mixture = [v.d2snd[node * 4 + dev, i].astype(F32) for i in range(4)]
-    for k, copy in reversed(d2):
-        copy.wait_recv()
+    for _, copy in reversed(d2):
+        copy.wait_recv()
+    for k in range(1, 16):
         for i in range(4):
             mixture[i] += v.d2rcv[k, i].astype(F32)
     for i in range(4):
@@ -372,8 +412,9 @@
     for k in far_z:
         d3.append((k, push("d3", k, v.d3snd.at[turn(z, k, 8)], v.d3rcv.at[k], at_z(k))))
     mixture = v.d3snd[z]
-    for k, copy in reversed(d3):
-        copy.wait_recv()
+    for _, copy in reversed(d3):
+        copy.wait_recv()
+    for k in range(1, 8):
         mixture += v.d3rcv[k]
     out_ref[...] = (own + mixture).astype(BF16)[:, :112]
 
@@ -385,13 +426,13 @@
            expert_weights, gate_weight, up_weight, down_weight):
     vmem, anywhere = pl.BlockSpec(memory_space=pltpu.VMEM), pl.BlockSpec(memory_space=pl.ANY)
     scratch = [pltpu.VMEM(shape, dtype) for _, shape, dtype in BUFFERS]
-    scratch.append(pltpu.SemaphoreType.DMA((22,)))
+    scratch.append(pltpu.SemaphoreType.DMA((27,)))
     for _, count in PAIRS:
         scratch += [pltpu.SemaphoreType.DMA((count,)), pltpu.SemaphoreType.DMA((count,))]
     return pl.pallas_call(
         kernel,
         out_shape=jax.ShapeDtypeStruct((8, 112), BF16),
-        in_specs=[vmem] * 5 + [anywhere] * 7,
+        in_specs=[anywhere] * 12,
         out_specs=vmem,
         scratch_shapes=scratch,
         compiler_params=pltpu.CompilerParams(

time: 59.8 us -> 57.2 us (0.957)
  Pallas kernels: 58.3 us -> 55.7 us
    pallas_call x1, Pallas kernels: 58.3 us -> 55.7 us  [shards(): pl.pallas_call(kernel, out_shape=jax.ShapeDtypeStruct((8, 112), BF16), in...]
where the time goes in v1:
time: 57.2 us; the launch traced here: 56.9 us
  Pallas kernels  55.7 us (97%)
  local copies, waits for them, and re-layouts  1.26 us (2%)
    pallas_call x1, Pallas kernels, shards(): pl.pallas_call(kernel, out_shape=jax.ShapeDtypeStruct((8, 112), BF16), in...  55.7 us
    unnamed x1, local copies, waits for them, and re-layouts  1.26 us

profile of v1, /device:TPU:2, one launch (start us, length us, event | category | flops | bytes accessed | tf_op | source)
XLA Modules:
  0.0 56.9 jit_solution(17354924550051997088)
XLA Ops:
  0.0 55.7 %layer.1 = bf16[8,112]{1,0:T(8,128)(2,1)} custom-call(s32[8,32]{1,0:T(8,128)} %ids_hbm.1, bf16[56,128]{1,0:T(8,128)(2,1)} %bitcast.7, s32[8,32]{1,0:T(8,128)} %bitcast.8, f32[8,32]{1,0:T(8,128)} %bitcast.9, bf16[8,7168]{1,0:T(8,128)(2,1)} %res_hbm.1, bf16[8,576,128]{2,1,0:T(8,128)(2,1)} %bitcast.6, bf16[8,576,256]{2,1,0:T(8,128)(2,1)} %bitcast.5, ...), custom_call_target="tpu_custom_call" | custom-call | tf_op jit(solution)/shard_map/layer/pallas_call | solution.py:432
  55.7 1.3 %copy.14 = bf16[8,112]{1,0:T(8,128)(2,1)} copy(bf16[8,112]{1,0:T(8,128)(2,1)} %layer.1) | data formatting | bytes 3584

commit v2 on v1

--- a/solution.py
+++ b/solution.py
@@ -14,7 +14,7 @@
 norm_eps = 1e-06
 
 PAIRS = (
-    ("a1", 8), ("s1", 8), ("s2", 8), ("a2", 8), ("a3", 8), ("b1", 8),
+    ("a1", 8), ("s1", 8), ("s2", 8), ("a2", 8), ("a3", 8), ("e1", 8), ("e2", 4), ("b1", 8),
     ("b2", 8), ("c1", 16), ("c2", 4), ("wd", 1), ("hid", 1), ("d2", 16), ("d3", 8),
 )
 BUFFERS = (
@@ -22,9 +22,10 @@
     ("res", (8, 7168), BF16), ("qv", (8, 576, 128), BF16), ("cv", (8, 576, 256), BF16), ("liftv", (2, 512, 128), BF16),
     ("wov", (256, 7168), BF16), ("wguv", (7168, 256), BF16), ("wdv", (128, 7168), BF16),
     ("keep", (8, 256), F32), ("probs", (8, 128, 256), BF16),
-    ("st1", (8, 16, 128), F32), ("st2", (8, 16, 128), F32), ("fcol", (128, 128), F32),
+    ("st1", (8, 16, 128), F32), ("st2", (8, 24, 128), F32), ("fcol", (128, 128), F32),
     ("a1own", (8, 64, 512), F32), ("a1snd", (8, 64, 512), BF16), ("a1rcv", (8, 64, 512), BF16),
-    ("a2snd", (4, 8, 16, 512), BF16), ("a2rcv", (4, 8, 16, 512), BF16),
+    ("a2snd", (4, 6, 16, 512), BF16), ("a2rcv", (4, 6, 16, 512), BF16),
+    ("e1snd", (8, 16, 512), BF16), ("e1rcv", (8, 16, 512), BF16), ("e2snd", (4, 16, 512), BF16), ("e2rcv", (4, 16, 512), BF16),
     ("a3snd", (8, 16, 512), BF16), ("a3rcv", (8, 16, 512), BF16),
     ("b1snd", (8, 16, 512), BF16), ("b1rcv", (8, 16, 512), BF16), ("part", (8, 16, 512), BF16),
     ("state", (32, 16, 512), BF16), ("normed", (4, 64, 512), BF16), ("gain", (8, 16, 512), F32),
@@ -197,7 +198,7 @@
             peak = jnp.maximum(peak, ref[i, :8, :])
         total = jnp.zeros((8, 128), F32)
         for i in range(8):
-            total += ref[i, 8:, :] * jnp.exp(ref[i, :8, :] - peak)
+            total += ref[i, 8:16, :] * jnp.exp(ref[i, :8, :] - peak)
         return peak, total
 
     def pair_top(x):
@@ -210,20 +211,31 @@
     v.fcol[...] = jnp.concatenate([here, there, jnp.zeros((112, 128), F32)], axis=0).T
 
     half = pl.ds(pl.multiple_of(core * 64, 64), 64)
+
+    def core_join(r):
+        both = v.fcol[half, r:r + 1] * v.a1own[r] + v.fcol[half, r + 8:r + 9] * v.a1rcv[r].astype(F32)
+        return both.astype(BF16)
+
     a2 = []
-    for r in range(8):
-        if r % 4 == 0:
-            for copy in a1[r:r + 4]:
-                copy.wait_recv()
-        both = v.fcol[half, r:r + 1] * v.a1own[r] + v.fcol[half, r + 8:r + 9] * v.a1rcv[r].astype(F32)
-        both = both.astype(BF16)
-        for x in range(4):
-            v.a2snd[x, r] = both[x * 16:x * 16 + 16]
-        if r % 4 == 3:
-            chunk = pl.ds(r - 3, 4)
-            for k in (2, 1, 3):
-                xt = turn(dev, k, 4)
-                a2.append(push("a2", k + r // 4 * 4, v.a2snd.at[xt, chunk], v.a2rcv.at[k, chunk], at(dev=xt)))
+    for c in range(2):
+        for copy in a1[3 * c:3 * c + 3]:
+            copy.wait_recv()
+        for r in range(3 * c, 3 * c + 3):
+            both = core_join(r)
+            for x in range(4):
+                v.a2snd[x, r] = both[x * 16:x * 16 + 16]
+        chunk = pl.ds(3 * c, 3)
+        for k in (2, 1, 3):
+            xt = turn(dev, k, 4)
+            a2.append(push("a2", k + c * 4, v.a2snd.at[xt, chunk], v.a2rcv.at[k, chunk], at(dev=xt)))
+    for copy in a1[6:]:
+        copy.wait_recv()
+    to_z = one_hot(
+        at_col == part_of(at_row, 1, 2) * 64 + part_of(at_row, 4, 4) * 16 + part_of(at_row, 16, 8) * 2 + part_of(at_row, 2, 2)
+    )
+    late = dot(to_z, jnp.concatenate([core_join(6), core_join(7)], axis=0))
+    v.e1snd[...] = late.astype(BF16).reshape(8, 16, 512)
+    e1 = [push("e1", k, v.e1snd.at[turn(z, k, 8)], v.e1rcv.at[k], at_z(k)) for k in far_z]
     ready(fetch_gain)
     for i in range(8):
         for t in range(4):
@@ -248,7 +260,8 @@
         copy.wait_recv()
     peak, total = joined(v.st1)
     v.st2[z, :8, :] = peak
-    v.st2[z, 8:, :] = total
+    v.st2[z, 8:16, :] = total
+    v.st2[z, 16:, :] = pair
     s2 = [push("s2", k, v.st2.at[z], v.st2.at[z], at_z(k)) for k in far_z]
 
     factors = [jnp.exp(pair_top(turn(dev, 4 - k, 4)) - peak) for k in range(4)]
@@ -257,29 +270,52 @@
     lay_out(range(2))
 
     sixteen = pl.ds(pl.multiple_of(core * 64 + dev * 16, 16), 16)
-    by_z = one_hot(at_col == part_of(at_row, 1, 8) * 16 + part_of(at_row, 16, 8) * 2 + part_of(at_row, 8, 2))
+    by_row, by_col = iota((128, 48), 0), iota((128, 48), 1)
     latents = jnp.zeros((128, 512), F32)
     for c in range(2):
         for copy in a2[3 * c:3 * c + 3]:
             copy.wait_recv()
         rows = []
-        for r in range(4 * c, 4 * c + 4):
+        for r in range(3 * c, 3 * c + 3):
             row = v.fcol[sixteen, r:r + 1] * v.a2snd[dev, r].astype(F32)
             for k in range(1, 4):
                 row += v.fcol[sixteen, k * 8 + r:k * 8 + r + 1] * v.a2rcv[k, r].astype(F32)
             rows.append(row.astype(BF16))
-        latents += dot(by_z[:, c * 64:c * 64 + 64], jnp.concatenate(rows, axis=0))
+        by_z = one_hot(by_col + c * 48 == part_of(by_row, 1, 8) * 16 + part_of(by_row, 16, 8) * 2 + part_of(by_row, 8, 2))
+        latents += dot(by_z, jnp.concatenate(rows, axis=0))
 
     v.a3snd[...] = latents.astype(BF16).reshape(8, 16, 512)
     a3 = []
     for k in far_z:
         zt = turn(z, k, 8)
         a3.append((k, push("a3", k, v.a3snd.at[zt], v.a3rcv.at[k], at_z(k))))
+    for copy in s2:
+        copy.wait_recv()
+    peak, total = joined(v.st2)
+
+    late_row, late_lane = iota((16, 128), 0), iota((16, 128), 1)
+    late_head = late_lane == core * 64 + part_of(late_row, 4, 4) * 16 + z * 2 + part_of(late_row, 2, 2)
+
+    def late_factor(zt):
+        factor = jnp.exp(v.st2[zt, 16:, :] - peak) / total
+        factor = jnp.where(part_of(late_row, 1, 2) == 0, factor[6:7], factor[7:8])
+        return jnp.sum(jnp.where(late_head, factor, 0.0), axis=1, keepdims=True)
+
+    late_factors = [late_factor(turn(z, 8 - k, 8)) for k in range(8)]
+    for copy in reversed(e1):
+        copy.wait_recv()
+    late = late_factors[0] * v.e1snd[z].astype(F32)
+    for k in range(1, 8):
+        late += late_factors[k] * v.e1rcv[k].astype(F32)
+    to_row, to_col = iota((64, 16), 0), iota((64, 16), 1)
+    to_x = one_hot(
+        (part_of(to_row, 1, 8) >= 6)
+        & (to_col == part_of(to_row, 16, 4) * 4 + part_of(to_row, 8, 2) * 2 + part_of(to_row, 1, 8) - 6)
+    )
+    v.e2snd[...] = dot(to_x, late.astype(BF16)).astype(BF16).reshape(4, 16, 512)
+    e2 = [push("e2", k, v.e2snd.at[turn(dev, k, 4)], v.e2rcv.at[k], at(dev=turn(dev, k, 4))) for k in (2, 1, 3)]
     lay_out(range(2, 5))
     ready(fetch_lift, fetch_wo)
-    for copy in s2:
-        copy.wait_recv()
-    peak, total = joined(v.st2)
 
     own_lane = iota((8, 128), 1) - (core * 64 + dev * 16 + z * 2)
 
@@ -294,6 +330,11 @@
         copy.wait_recv()
     for k in range(1, 8):
         summed += factors[k] * v.a3rcv[k].astype(F32)
+    for copy in e2:
+        copy.wait_recv()
+    summed += v.e2snd[dev].astype(F32)
+    for k in range(1, 4):
+        summed += v.e2rcv[k].astype(F32)
     own_heads = summed.astype(BF16)
     values = jnp.concatenate([dot(own_heads, v.liftv[0])[:8], dot(own_heads, v.liftv[1])[8:]], axis=1).astype(BF16)
 

time: 57.2 us -> 56 us (0.979)
  Pallas kernels: 55.7 us -> 54.6 us
    pallas_call x1, Pallas kernels: 55.7 us -> 54.6 us  [shards(): pl.pallas_call(kernel, out_shape=jax.ShapeDtypeStruct((8, 112), BF16), in...]
where the time goes in v2:
time: 56 us; the launch traced here: 55.9 us
  Pallas kernels  54.6 us (98%)
  local copies, waits for them, and re-layouts  1.26 us (2%)
    pallas_call x1, Pallas kernels, shards(): pl.pallas_call(kernel, out_shape=jax.ShapeDtypeStruct((8, 112), BF16), in...  54.6 us
    unnamed x1, local copies, waits for them, and re-layouts  1.26 us

profile of v2, /device:TPU:2, one launch (start us, length us, event | category | flops | bytes accessed | tf_op | source)
XLA Modules:
  0.0 55.9 jit_solution(12738015497310793586)
XLA Ops:
  0.0 54.6 %layer.1 = bf16[8,112]{1,0:T(8,128)(2,1)} custom-call(s32[8,32]{1,0:T(8,128)} %ids_hbm.1, bf16[56,128]{1,0:T(8,128)(2,1)} %bitcast.7, s32[8,32]{1,0:T(8,128)} %bitcast.8, f32[8,32]{1,0:T(8,128)} %bitcast.9, bf16[8,7168]{1,0:T(8,128)(2,1)} %res_hbm.1, bf16[8,576,128]{2,1,0:T(8,128)(2,1)} %bitcast.6, bf16[8,576,256]{2,1,0:T(8,128)(2,1)} %bitcast.5, ...), custom_call_target="tpu_custom_call" | custom-call | tf_op jit(solution)/shard_map/layer/pallas_call | solution.py:473
  54.6 1.3 %copy.14 = bf16[8,112]{1,0:T(8,128)(2,1)} copy(bf16[8,112]{1,0:T(8,128)(2,1)} %layer.1) | data formatting | bytes 3584

commit v3 on v2

--- a/solution.py
+++ b/solution.py
@@ -99,6 +99,12 @@
         sent.append(copy)
         return copy
 
+    def settle(flying):
+        done = len(sent) - flying
+        for copy in sent[:done]:
+            copy.wait_send()
+        del sent[:done]
+
     far_z, far_g = (4, 3, 5, 2, 6, 1, 7), (2, 6, 1, 3, 5, 7, 4)
 
     def hops(i, j):
@@ -371,6 +377,7 @@
     keep_wd = pltpu.make_async_copy(v.laid.at[core], v.down.at[mine_rows], local.at[21])
     keep_wd.start()
     fetches.append(keep_wd)
+    settle(8)
     ready(fetch_wg, fetch_wu)
     for copy in b2:
         copy.wait_recv()
@@ -387,6 +394,7 @@
     ready(fetch_eid, fetch_ew)
     coef = jnp.sum(jnp.where(v.eid[...] == expert, v.ew[...], 0.0), axis=0, keepdims=True)
     coef = jnp.sum(jnp.where(iota((32, 32), 0) == iota((32, 32), 1), coef, 0.0), axis=1, keepdims=True)
+    settle(16)
     for i in (0, 1, 3, 2):
         for j in range(4):
             if i + j > 0:
@@ -440,6 +448,7 @@
     for i, j in far_xy:
         yt, xt = turn(node, i, 4), turn(dev, j, 4)
         d2.append((i * 4 + j, push("d2", i * 4 + j, v.d2snd.at[yt * 4 + xt], v.d2rcv.at[i * 4 + j], at(node=yt, dev=xt))))
+    settle(15)
     mixture = [v.d2snd[node * 4 + dev, i].astype(F32) for i in range(4)]
     for _, copy in reversed(d2):
         copy.wait_recv()
@@ -452,6 +461,7 @@
     d3 = []
     for k in far_z:
         d3.append((k, push("d3", k, v.d3snd.at[turn(z, k, 8)], v.d3rcv.at[k], at_z(k))))
+    settle(7)
     mixture = v.d3snd[z]
     for _, copy in reversed(d3):
         copy.wait_recv()

time: 56 us -> 55.8 us (level)
  no operation moved by 1% of the time
where the time goes in v3:
time: 55.8 us; the launch traced here: 55.7 us
  Pallas kernels  54.4 us (97%)
  local copies, waits for them, and re-layouts  1.26 us (2%)
    pallas_call x1, Pallas kernels, shards(): pl.pallas_call(kernel, out_shape=jax.ShapeDtypeStruct((8, 112), BF16), in...  54.4 us
    unnamed x1, local copies, waits for them, and re-layouts  1.26 us

profile of v3, /device:TPU:2, one launch (start us, length us, event | category | flops | bytes accessed | tf_op | source)
XLA Modules:
  0.0 55.7 jit_solution(3467340425613577720)
XLA Ops:
  0.0 54.4 %layer.1 = bf16[8,112]{1,0:T(8,128)(2,1)} custom-call(s32[8,32]{1,0:T(8,128)} %ids_hbm.1, bf16[56,128]{1,0:T(8,128)(2,1)} %bitcast.7, s32[8,32]{1,0:T(8,128)} %bitcast.8, f32[8,32]{1,0:T(8,128)} %bitcast.9, bf16[8,7168]{1,0:T(8,128)(2,1)} %res_hbm.1, bf16[8,576,128]{2,1,0:T(8,128)(2,1)} %bitcast.6, bf16[8,576,256]{2,1,0:T(8,128)(2,1)} %bitcast.5, ...), custom_call_target="tpu_custom_call" | custom-call | tf_op jit(solution)/shard_map/layer/pallas_call | solution.py:483
  54.4 1.3 %copy.14 = bf16[8,112]{1,0:T(8,128)(2,1)} copy(bf16[8,112]{1,0:T(8,128)(2,1)} %layer.1) | data formatting | bytes 3584
